TPU v7x, 256 devices: a whole 4x4x8 slice. The times are simulated.
256 devices in a mesh: section: 8 (over y, core), seq: 32 (over x, z).
Axes of the slice: x: 4, y: 4, z: 8, core: 2. Of those that a mesh axis runs over, the one named last changes fastest.
Arguments:
- queries: bfloat16 [8, 8192, 2560], P('section', 'seq'), may hold values from -200 to 200
- keys: bfloat16 [8, 8192, 512], P('section', 'seq'), may hold values from -4 to 4
- values: bfloat16 [8, 8192, 512], P('section', 'seq'), may hold values from -6 to 6
- lengths: int32 [8, 64], P('section'), may hold values from 1 to 1024, 8192 in all within a row
Outputs:
- handed: bfloat16 [8, 8192, 2560], P('section', 'seq')
Inputs may be any that keep to these rules, and one draw needn't show every extreme that they name: `lengths`: each row sums to 8192; its longest episode has exactly 1024 positions.
All inputs are finite; a program needn't handle non-finite values.
Results may differ from a plain program's by a relative error of at most 0.003.
Values may be sent and summed in bfloat16 or wider, within the bound.
No kernel may reach another device: no remote copies, remote signals or barrier semaphores. Data moves between devices by JAX's collectives and lax.ppermute only.
A program may use at most 128 MiB of HBM per device.

v0:
```python
from functools import partial

import jax
import jax.numpy as jnp
from jax import lax
from jax.sharding import PartitionSpec as P

HDIM = 128
REACH = 4


LOWEST = -1e30


def passed_along(value, axis, steps):
    count = lax.axis_size(axis)
    first, last = (max(0, -steps), min(count, count - steps))
    return lax.ppermute(value, axis, [(source, source + steps) for source in range(first, last)])


def passed_along_2(block, axis, distance):
    devices = range(lax.axis_size(axis))
    route = [((i - distance) % len(devices), i) for i in devices]
    return lax.ppermute(block, axis, route)


def first_starts(begins, positions):
    inside = begins[None, :] <= positions[:, None]
    return jnp.max(jnp.where(inside, begins[None, :], 0), axis=1)


def live_tiles(begins, index, height):
    opening = first_starts(begins, jnp.reshape(index * height, (1,)))[0]
    backs = jnp.arange(1, REACH + 1, dtype=jnp.int32)
    usable = (index - backs >= 0) & (opening < (index - backs + 1) * height)
    return jnp.sum(usable.astype(jnp.int32))


def tile_terms(query_block, pair_block, query_pos, key_pos, query_start):
    height = query_block.shape[0]
    kv_width = pair_block.shape[1] // 2
    kv_heads = kv_width // HDIM
    per_group = query_block.shape[1] // kv_width
    query_grid = query_block.reshape(height, kv_heads, per_group, HDIM)
    key_grid = pair_block[:, :kv_width].reshape(height, kv_heads, HDIM)
    value_grid = pair_block[:, kv_width:].reshape(height, kv_heads, HDIM)
    scores = jnp.einsum(
        "qagd,kad->agqk", query_grid, key_grid, preferred_element_type=jnp.float32
    ) * HDIM ** (-0.5)
    visible = (key_pos[None, :] <= query_pos[:, None]) & (key_pos[None, :] >= query_start[:, None])
    tile_max = jnp.max(jnp.where(visible, scores, LOWEST), axis=3)
    weights = jnp.where(visible, jnp.exp(scores - tile_max[..., None]), 0.0)
    tile_sum = jnp.sum(weights, axis=3)
    tile_out = jnp.einsum(
        "agqk,kad->qagd",
        weights.astype(jnp.bfloat16),
        value_grid,
        preferred_element_type=jnp.float32,
    )
    return (tile_out, tile_max, tile_sum)


def empty_terms(height, kv_heads, per_group):
    return (
        jnp.zeros((height, kv_heads, per_group, HDIM), jnp.float32),
        jnp.full((kv_heads, per_group, height), LOWEST, jnp.float32),
        jnp.zeros((kv_heads, per_group, height), jnp.float32),
    )


def merge_terms(terms):
    highest = terms[0][1]
    for item in terms[1:]:
        highest = jnp.maximum(highest, item[1])
    total_out = jnp.zeros_like(terms[0][0])
    total_sum = jnp.zeros_like(terms[0][2])
    for tile_out, tile_max, tile_sum in terms:
        factor = jnp.exp(tile_max - highest)
        total_out = total_out + tile_out * jnp.transpose(factor, (2, 0, 1))[..., None]
        total_sum = total_sum + tile_sum * factor
    return (total_out, highest, total_sum)


def far_terms(query_block, earlier, index, starts, lower_cut, upper_cut):
    height = query_block.shape[0]
    kv_heads = earlier[0].shape[1] // (2 * HDIM)
    per_group = query_block.shape[1] // (kv_heads * HDIM)
    query_pos = index * height + jnp.arange(height, dtype=jnp.int32)
    terms = []
    for back in range(1, REACH + 1):
        key_pos = (index - back) * height + jnp.arange(height, dtype=jnp.int32)
        wanted = (back > lower_cut) & (back <= upper_cut)
        terms.append(
            lax.cond(
                wanted,
                partial(tile_terms, query_block, earlier[back - 1], query_pos, key_pos, starts),
                partial(empty_terms, height, kv_heads, per_group),
            )
        )
    return terms


def body(queries, keys, values, lengths):
    query_block = queries[0]
    height = query_block.shape[0]
    own_index = lax.axis_index("seq")
    sizes_row = lengths[0]
    begins = jnp.cumsum(sizes_row, dtype=jnp.int32) - sizes_row
    positions = own_index * height + jnp.arange(height, dtype=jnp.int32)
    starts = first_starts(begins, positions)
    own_pair = jnp.concatenate([keys[0], values[0]], axis=1)
    earlier = [passed_along(own_pair, "seq", back) for back in range(1, REACH + 1)]
    own_count = live_tiles(begins, own_index, height)
    diagonal = tile_terms(query_block, own_pair, positions, positions, starts)
    total = merge_terms(
        [diagonal] + far_terms(query_block, earlier, own_index, starts, 0, own_count)
    )
    finished = total[0] / jnp.transpose(total[2], (2, 0, 1))[..., None]
    attended = finished.astype(jnp.bfloat16).reshape(height, -1)
    return passed_along_2(attended[None], "section", 1)


def solution(mesh):
    return jax.shard_map(
        body,
        mesh=mesh,
        in_specs=(
            P("section", "seq", None),
            P("section", "seq", None),
            P("section", "seq", None),
            P("section", None),
        ),
        out_specs=P("section", "seq", None),
        check_vma=False,
    )
```

profile of v0, /device:TPU:68, one launch (start us, length us, event | category | flops | bytes accessed | tf_op | source)
XLA Modules:
  0.0 145.8 jit_solution(12723003551657509938)
XLA Ops:
  1.1 1.1 copy.75
  3.0 7.3 %collective-permute-start.3 = (bf16[256,1024]{0,1:T(8,128)(2,1)}, bf16[256,1024]{0,1:T(8,128)(2,1)S(1)}, u32[]{:S(2)}, u32[]{:S(2)}) collective-permute-start(bf16[256,1024]{0,1:T(8,128)(2,1)} %pad_maximum_fusion), channel_id=1, source_target_pairs={{0,4},{1,5},{2,6},{3,7},{4,8},{5,9},{6,10},{7,11},{8,12},{9,13},{1... | collective-permute-start | bytes 1572872 | tf_op jit(solution)/shard_map/ppermute | solution.py:18
  10.3 1.9 %collective-permute-start.2 = (bf16[256,1024]{0,1:T(8,128)(2,1)}, bf16[256,1024]{0,1:T(8,128)(2,1)}, u32[]{:S(2)}, u32[]{:S(2)}) collective-permute-start(bf16[256,1024]{0,1:T(8,128)(2,1)} %pad_maximum_fusion), channel_id=1, source_target_pairs={{0,3},{1,4},{2,5},{3,6},{4,7},{5,8},{6,9},{7,10},{8,11},{9,12},{10... | collective-permute-start | bytes 1572872 | tf_op jit(solution)/shard_map/ppermute | solution.py:18
  12.2 5.0 %collective-permute-start.1 = (bf16[256,1024]{0,1:T(8,128)(2,1)}, bf16[256,1024]{0,1:T(8,128)(2,1)}, u32[]{:S(2)}, u32[]{:S(2)}) collective-permute-start(bf16[256,1024]{0,1:T(8,128)(2,1)} %pad_maximum_fusion), channel_id=1, source_target_pairs={{0,2},{1,3},{2,4},{3,5},{4,6},{5,7},{6,8},{7,9},{8,10},{9,11},{10,... | collective-permute-start | bytes 1572872 | tf_op jit(solution)/shard_map/ppermute | solution.py:18
  17.2 5.0 %collective-permute-start = (bf16[256,1024]{0,1:T(8,128)(2,1)}, bf16[256,1024]{0,1:T(8,128)(2,1)}, u32[]{:S(2)}, u32[]{:S(2)}) collective-permute-start(bf16[256,1024]{0,1:T(8,128)(2,1)} %pad_maximum_fusion), channel_id=1, source_target_pairs={{0,1},{1,2},{2,3},{3,4},{4,5},{5,6},{6,7},{7,8},{8,9},{9,10},{10,1... | collective-permute-start | bytes 1572872 | tf_op jit(solution)/shard_map/ppermute | solution.py:18
  24.2 1.3 subtract_bitcast_fusion
  25.7 1.6 %copy.70 = bf16[1,256,2560]{1,2,0:T(8,128)(2,1)S(1)} copy(bf16[1,256,2560]{2,1,0:T(8,128)(2,1)} %param.12) | data formatting | bytes 2621440 | tf_op args[0]
  28.3 2.3 %copy-done = f32[4,256,256,5]{2,1,3,0:T(8,128)} copy-done((f32[4,256,256,5]{2,1,3,0:T(8,128)}, f32[4,256,256,5]{2,1,3,0:T(8,128)S(1)}, u32[]{:S(2)}) %copy-start) | copy-done | bytes 5242904
  30.6 2.7 %fusion.69 = f32[4,5,256,128]{2,3,1,0:T(8,128)} fusion(bf16[256,4,128,1]{0,2,3,1:T(8,128)(2,1)S(1)} %bitcast.189, f32[4,256,256,5]{2,1,3,0:T(8,128)S(1)} %get-tuple-element.259, f32[4,5,256]{2,1,0:T(8,128)S(1)} %get-tuple-element.258, pred[256,256]{0,1:T(8,128)(4,1)S(1)} %compare_and_fusion.4), kind=kOutput, calls=%fused_computation.75 | convolution fusion | flops 340787200 | bytes 8212480 | tf_op jit(solution)/shard_map/agqk,kad->qagd/dot_general | solution.py:54
  33.3 1.3 fusion.89
  37.2 3.6 %fusion.67 = f32[4,5,256]{2,1,0:T(8,128)S(1)} fusion(f32[4,256,256,5]{2,1,3,0:T(8,128)} %copy-done, f32[4,5,256]{2,1,0:T(8,128)S(1)} %get-tuple-element.258, pred[256,256]{0,1:T(8,128)(4,1)S(1)} %compare_and_fusion.4), kind=kLoop, calls=%fused_computation.73 | loop fusion | flops 5237760 | bytes 5349376 | tf_op jit(solution)/shard_map/reduce_sum | solution.py:53
  40.8 2.5 %conditional.7 = (f32[4,5,256]{2,1,0:T(8,128)}, f32[4,5,256]{2,1,0:T(8,128)S(1)}, f32[256,4,5,128]{0,3,2,1:T(8,128)}) conditional(s32[]{:T(128)} %convert_element_type.38, () %tuple.43, (s32[]{:T(128)}, s32[256]{0:T(256)S(1)}, s32[256]{0:T(256)S(1)}, bf16[256,1024]{0,1:T(8,128)(2,1)S(1)}, bf16[1,256,2560]{2,1,0:T(8,128)(2,1)S(1)}, ...), branch_computations={%region_17.18_spmd, %region_18.21_spmd.clone} | conditional | flops 685693184 | bytes 29447220 | solution.py:94
  41.4 1.9 %broadcast.101.clone = f32[256,4,5,128]{0,3,2,1:T(8,128)} broadcast(f32[]{:T(128)} %constant.54.clone), dimensions={} | broadcast | bytes 2621444 | tf_op jit(solution)/shard_map/broadcast.33
  43.2 29.5 %collective-permute-done.2 = bf16[256,1024]{0,1:T(8,128)(2,1)} collective-permute-done((bf16[256,1024]{0,1:T(8,128)(2,1)}, bf16[256,1024]{0,1:T(8,128)(2,1)}, u32[]{:S(2)}, u32[]{:S(2)}) %collective-permute-start.2) | collective-permute-done | bytes 524320 | tf_op jit(solution)/shard_map/ppermute | solution.py:18
  72.7 12.4 %conditional.6 = (f32[4,5,256]{2,1,0:T(8,128)}, f32[4,5,256]{2,1,0:T(8,128)S(1)}, f32[256,4,5,128]{0,3,2,1:T(8,128)}) conditional(s32[]{:T(128)} %convert_element_type.37, () %tuple.41, (s32[]{:T(128)}, s32[256]{0:T(256)S(1)}, s32[256]{0:T(256)S(1)}, bf16[256,1024]{0,1:T(8,128)(2,1)}, bf16[1,256,2560]{2,1,0:T(8,128)(2,1)S(1)}, ...), branch_computations={%region_13.14_spmd, %region_14.17_spmd.clone} | conditional | flops 685693184 | bytes 29447220 | solution.py:94
  74.6 1.6 %fusion.32 = (f32[4,5,256]{2,1,0:T(8,128)}, f32[4,256,256,5]{2,1,3,0:T(8,128)S(1)}) fusion(pred[256,256]{0,1:T(8,128)(4,1)S(1)} %compare_and_fusion.2, bf16[256,4,128,1]{0,2,3,1:T(8,128)(2,1)S(1)} %bitcast.197, bf16[256,4,5,128]{0,3,2,1:T(8,128)(2,1)S(1)} %bitcast.185), kind=kOutput, calls=%fused_computation.36 | convolution fusion | flops 339471360 | bytes 6901760 | tf_op jit(solution)/shard_map/cond/branch_1_fun/qagd,kad->agqk/dot_general | solution.py:47
  76.2 1.8 %fusion.35 = f32[4,5,256]{2,1,0:T(8,128)S(1)} fusion(f32[4,256,256,5]{2,1,3,0:T(8,128)S(1)} %get-tuple-element.246, f32[4,5,256]{2,1,0:T(8,128)} %get-tuple-element.269, pred[256,256]{0,1:T(8,128)(4,1)S(1)} %compare_and_fusion.2), kind=kLoop, calls=%fused_computation.39 | loop fusion | flops 5237760 | bytes 5349376 | tf_op jit(solution)/shard_map/cond/branch_1_fun/reduce_sum | solution.py:53
  78.0 3.9 %fusion.43 = f32[256,4,5,128]{3,0,2,1:T(8,128)} fusion(bf16[256,4,128,1]{0,2,3,1:T(8,128)(2,1)S(1)} %bitcast.191, f32[4,256,256,5]{2,1,3,0:T(8,128)S(1)} %get-tuple-element.246, f32[4,5,256]{2,1,0:T(8,128)} %get-tuple-element.269, pred[256,256]{0,1:T(8,128)(4,1)S(1)} %compare_and_fusion.2), kind=kOutput, calls=%fused_computation.46 | convolution fusion | flops 340787200 | bytes 8212480 | tf_op jit(solution)/shard_map/cond/branch_1_fun/agqk,kad->qagd/dot_general | solution.py:54
  81.9 3.3 %copy.130 = f32[256,4,5,128]{0,3,2,1:T(8,128)} copy(f32[256,4,5,128]{3,0,2,1:T(8,128)} %fusion.43) | data formatting | bytes 5242880 | tf_op jit(solution)/shard_map/cond | solution.py:94
  85.1 7.2 %collective-permute-done.1 = bf16[256,1024]{0,1:T(8,128)(2,1)} collective-permute-done((bf16[256,1024]{0,1:T(8,128)(2,1)}, bf16[256,1024]{0,1:T(8,128)(2,1)}, u32[]{:S(2)}, u32[]{:S(2)}) %collective-permute-start.1) | collective-permute-done | bytes 524320 | tf_op jit(solution)/shard_map/ppermute | solution.py:18
  92.3 12.4 %conditional.5 = (f32[4,5,256]{2,1,0:T(8,128)}, f32[4,5,256]{2,1,0:T(8,128)S(1)}, f32[256,4,5,128]{0,3,2,1:T(8,128)}) conditional(s32[]{:T(128)} %convert_element_type.36, () %tuple.39, (s32[]{:T(128)}, s32[256]{0:T(256)S(1)}, s32[256]{0:T(256)S(1)}, bf16[256,1024]{0,1:T(8,128)(2,1)}, bf16[1,256,2560]{2,1,0:T(8,128)(2,1)S(1)}, ...), branch_computations={%region_9.10_spmd, %region_10.13_spmd.clone} | conditional | flops 685693184 | bytes 29447220 | solution.py:94
  94.1 1.6 %fusion.16 = (f32[4,5,256]{2,1,0:T(8,128)}, f32[4,256,256,5]{2,1,3,0:T(8,128)S(1)}) fusion(pred[256,256]{0,1:T(8,128)(4,1)S(1)} %compare_and_fusion.1, bf16[256,4,128,1]{0,2,3,1:T(8,128)(2,1)S(1)} %bitcast.198, bf16[256,4,5,128]{0,3,2,1:T(8,128)(2,1)S(1)} %bitcast.186), kind=kOutput, calls=%fused_computation.19 | convolution fusion | flops 339471360 | bytes 6901760 | tf_op jit(solution)/shard_map/cond/branch_1_fun/qagd,kad->agqk/dot_general | solution.py:47
  95.7 1.8 %fusion.19 = f32[4,5,256]{2,1,0:T(8,128)S(1)} fusion(f32[4,256,256,5]{2,1,3,0:T(8,128)S(1)} %get-tuple-element.242, f32[4,5,256]{2,1,0:T(8,128)} %get-tuple-element.275, pred[256,256]{0,1:T(8,128)(4,1)S(1)} %compare_and_fusion.1), kind=kLoop, calls=%fused_computation.22 | loop fusion | flops 5237760 | bytes 5349376 | tf_op jit(solution)/shard_map/cond/branch_1_fun/reduce_sum | solution.py:53
  97.6 3.9 %fusion.27 = f32[256,4,5,128]{3,0,2,1:T(8,128)} fusion(bf16[256,4,128,1]{0,2,3,1:T(8,128)(2,1)S(1)} %bitcast.192, f32[4,256,256,5]{2,1,3,0:T(8,128)S(1)} %get-tuple-element.242, f32[4,5,256]{2,1,0:T(8,128)} %get-tuple-element.275, pred[256,256]{0,1:T(8,128)(4,1)S(1)} %compare_and_fusion.1), kind=kOutput, calls=%fused_computation.29 | convolution fusion | flops 340787200 | bytes 8212480 | tf_op jit(solution)/shard_map/cond/branch_1_fun/agqk,kad->qagd/dot_general | solution.py:54
  101.5 3.2 %copy.128 = f32[256,4,5,128]{0,3,2,1:T(8,128)} copy(f32[256,4,5,128]{3,0,2,1:T(8,128)} %fusion.27) | data formatting | bytes 5242880 | tf_op jit(solution)/shard_map/cond | solution.py:94
  104.7 12.5 %conditional.4 = (f32[4,5,256]{2,1,0:T(8,128)}, f32[4,5,256]{2,1,0:T(8,128)S(1)}, f32[256,4,5,128]{0,3,2,1:T(8,128)}) conditional(s32[]{:T(128)} %convert_element_type.35, () %tuple.37, (s32[]{:T(128)}, s32[256]{0:T(256)S(1)}, s32[256]{0:T(256)S(1)}, bf16[256,1024]{0,1:T(8,128)(2,1)}, bf16[1,256,2560]{2,1,0:T(8,128)(2,1)S(1)}, ...), branch_computations={%region_5.6_spmd, %region_6.9_spmd.clone} | conditional | flops 685693184 | bytes 29447220 | solution.py:94
  106.7 1.6 %fusion = (f32[4,5,256]{2,1,0:T(8,128)}, f32[4,256,256,5]{2,1,3,0:T(8,128)S(1)}) fusion(pred[256,256]{0,1:T(8,128)(4,1)S(1)} %compare_and_fusion, bf16[256,4,128,1]{0,2,3,1:T(8,128)(2,1)S(1)} %bitcast.199, bf16[256,4,5,128]{0,3,2,1:T(8,128)(2,1)S(1)} %bitcast.187), kind=kOutput, calls=%fused_computation.2 | convolution fusion | flops 339471360 | bytes 6901760 | tf_op jit(solution)/shard_map/cond/branch_1_fun/qagd,kad->agqk/dot_general | solution.py:47
  108.3 1.8 %fusion.3 = f32[4,5,256]{2,1,0:T(8,128)S(1)} fusion(f32[4,256,256,5]{2,1,3,0:T(8,128)S(1)} %get-tuple-element.238, f32[4,5,256]{2,1,0:T(8,128)} %get-tuple-element.281, pred[256,256]{0,1:T(8,128)(4,1)S(1)} %compare_and_fusion), kind=kLoop, calls=%fused_computation.5 | loop fusion | flops 5237760 | bytes 5349376 | tf_op jit(solution)/shard_map/cond/branch_1_fun/reduce_sum | solution.py:53
  110.1 3.9 %fusion.11 = f32[256,4,5,128]{3,0,2,1:T(8,128)} fusion(bf16[256,4,128,1]{0,2,3,1:T(8,128)(2,1)S(1)} %bitcast.193, f32[4,256,256,5]{2,1,3,0:T(8,128)S(1)} %get-tuple-element.238, f32[4,5,256]{2,1,0:T(8,128)} %get-tuple-element.281, pred[256,256]{0,1:T(8,128)(4,1)S(1)} %compare_and_fusion), kind=kOutput, calls=%fused_computation.12 | convolution fusion | flops 340787200 | bytes 8212480 | tf_op jit(solution)/shard_map/cond/branch_1_fun/agqk,kad->qagd/dot_general | solution.py:54
  114.0 3.2 %copy.126 = f32[256,4,5,128]{0,3,2,1:T(8,128)} copy(f32[256,4,5,128]{3,0,2,1:T(8,128)} %fusion.11) | data formatting | bytes 5242880 | tf_op jit(solution)/shard_map/cond | solution.py:94
  118.9 6.8 %fusion.79 = bf16[256,4,5,128]{0,3,2,1:T(8,128)(2,1)S(1)} fusion(f32[256,4,5,128]{0,3,2,1:T(8,128)} %get-tuple-element.232, f32[256,4,5,128]{0,3,2,1:T(8,128)} %get-tuple-element.231, f32[256,4,5,128]{0,3,2,1:T(8,128)} %get-tuple-element.230, f32[256,4,5,128]{0,3,2,1:T(8,128)} %get-tuple-element.229, f32[4,5,256,128]{2,3,1,0:T(8,128)} %fusion.69, ...), kind=kLoop, calls=%fused_computation.85 | loop fusion | flops 7208960 | bytes 14540800 | tf_op jit(solution)/shard_map/convert_element_type | solution.py:119
  126.5 18.2 %collective-permute-done.4 = bf16[1,256,2560]{2,1,0:T(8,128)(2,1)S(1)} collective-permute-done((bf16[1,256,2560]{2,1,0:T(8,128)(2,1)S(1)}, bf16[1,256,2560]{2,1,0:T(8,128)(2,1)S(1)}, u32[]{:S(2)}, u32[]{:S(2)}) %collective-permute-start.4) | collective-permute-done | bytes 1310752 | tf_op jit(solution)/shard_map/ppermute | solution.py:24
  (36 shorter events, 14.6 us)
Async XLA Ops:
  3.0 37.7 %collective-permute-start.3 = (bf16[256,1024]{0,1:T(8,128)(2,1)}, bf16[256,1024]{0,1:T(8,128)(2,1)S(1)}, u32[]{:S(2)}, u32[]{:S(2)}) collective-permute-start(bf16[256,1024]{0,1:T(8,128)(2,1)} %pad_maximum_fusion), channel_id=1, source_target_pairs={{0,4},{1,5},{2,6},{3,7},{4,8},{5,9},{6,10},{7,11},{8,12},{9,13},{1... | collective-permute-start | bytes 1572872 | tf_op jit(solution)/shard_map/ppermute | solution.py:18
  10.3 62.4 %collective-permute-start.2 = (bf16[256,1024]{0,1:T(8,128)(2,1)}, bf16[256,1024]{0,1:T(8,128)(2,1)}, u32[]{:S(2)}, u32[]{:S(2)}) collective-permute-start(bf16[256,1024]{0,1:T(8,128)(2,1)} %pad_maximum_fusion), channel_id=1, source_target_pairs={{0,3},{1,4},{2,5},{3,6},{4,7},{5,8},{6,9},{7,10},{8,11},{9,12},{10... | collective-permute-start | bytes 1572872 | tf_op jit(solution)/shard_map/ppermute | solution.py:18
  12.2 80.1 %collective-permute-start.1 = (bf16[256,1024]{0,1:T(8,128)(2,1)}, bf16[256,1024]{0,1:T(8,128)(2,1)}, u32[]{:S(2)}, u32[]{:S(2)}) collective-permute-start(bf16[256,1024]{0,1:T(8,128)(2,1)} %pad_maximum_fusion), channel_id=1, source_target_pairs={{0,2},{1,3},{2,4},{3,5},{4,6},{5,7},{6,8},{7,9},{8,10},{9,11},{10,... | collective-permute-start | bytes 1572872 | tf_op jit(solution)/shard_map/ppermute | solution.py:18
  17.2 87.5 %collective-permute-start = (bf16[256,1024]{0,1:T(8,128)(2,1)}, bf16[256,1024]{0,1:T(8,128)(2,1)}, u32[]{:S(2)}, u32[]{:S(2)}) collective-permute-start(bf16[256,1024]{0,1:T(8,128)(2,1)} %pad_maximum_fusion), channel_id=1, source_target_pairs={{0,1},{1,2},{2,3},{3,4},{4,5},{5,6},{6,7},{7,8},{8,9},{9,10},{10,1... | collective-permute-start | bytes 1572872 | tf_op jit(solution)/shard_map/ppermute | solution.py:18
  28.3 2.3 %copy-start = (f32[4,256,256,5]{2,1,3,0:T(8,128)}, f32[4,256,256,5]{2,1,3,0:T(8,128)S(1)}, u32[]{:S(2)}) copy-start(f32[4,256,256,5]{2,1,3,0:T(8,128)S(1)} %get-tuple-element.259) | copy-start | bytes 15728644
  30.6 10.1 %copy-start.1 = (bf16[1,256,2560]{2,1,0:T(8,128)(2,1)S(1)}, bf16[1,256,2560]{2,1,0:T(8,128)(2,1)}, u32[]{:S(2)}) copy-start(bf16[1,256,2560]{2,1,0:T(8,128)(2,1)} %param.12) | copy-start | bytes 3932164
  126.5 18.3 %collective-permute-start.4 = (bf16[1,256,2560]{2,1,0:T(8,128)(2,1)S(1)}, bf16[1,256,2560]{2,1,0:T(8,128)(2,1)S(1)}, u32[]{:S(2)}, u32[]{:S(2)}) collective-permute-start(bf16[1,256,2560]{2,1,0:T(8,128)(2,1)S(1)} %copy.85), channel_id=1, source_target_pairs={{224,0},{0,32},{32,64},{64,96},{96,128},{128,160},{160,192},{192,2... | collective-permute-start | bytes 3932168 | tf_op jit(solution)/shard_map/ppermute | solution.py:24
where the time goes:
time: 147 us; the launch traced here: 146 us
  waiting for transfers between devices  54.9 us (37%)
  local copies, waits for them, and re-layouts  26.1 us (18%)
  other arithmetic  22.5 us (15%)
  matrix products  20.2 us (14%)
  starting transfers between devices  19.3 us (13%)
  between operations  2.7 us (2%)
    ppermute x4, waiting for transfers between devices, passed_along(): lax.ppermute(value, axis, [(source, source + steps) for source in range(f...  36.7 us
    ppermute x4, starting transfers between devices, passed_along(): lax.ppermute(value, axis, [(source, source + steps) for source in range(f...  19.2 us
    ppermute x1, waiting for transfers between devices, passed_along_2(): return lax.ppermute(block, axis, route)  18.2 us
    dot_general x4, matrix products, tile_terms(): jnp.einsum('agqk,kad->qagd', weights.astype(jnp.bfloat16), value_grid, pr...  14.4 us
    cond x3, local copies, waits for them, and re-layouts, far_terms(): lax.cond(wanted, partial(tile_terms, query_block, earlier[back - 1], quer...  9.67 us
    reduce_sum x4, other arithmetic, tile_terms(): tile_sum = jnp.sum(weights, axis=3)  9.05 us
    convert_element_type x1, other arithmetic, body(): attended = finished.astype(jnp.bfloat16).reshape(height, -1)  6.84 us
    unnamed x7, local copies, waits for them, and re-layouts  6.04 us
  transfers between devices with their start and end apart: 5, of which 3 were waited for; matrix products, arithmetic and copies ran while one was open for 28% of the time, Pallas kernels for 0%

commit v1 on v0

v1 whole, which is shorter than its diff:
```python
from functools import partial

import jax
import jax.numpy as jnp
from jax import lax
from jax.experimental import pallas as pl
from jax.experimental.pallas import tpu as pltpu
from jax.sharding import PartitionSpec as P

HDIM = 128
KV_HEADS = 4
GROUP = 5
REACH = 4
LOWEST = -1e30
SCALE = HDIM**-0.5 * 1.4426950408889634


def moved(value, route):
    sections, blocks = lax.axis_size("section"), lax.axis_size("seq")
    pairs = []
    for s in range(sections):
        for b in range(blocks):
            s2, b2 = route(s, b)
            pairs.append((s * blocks + b, (s2 % sections) * blocks + b2 % blocks))
    return lax.ppermute(value, ("section", "seq"), pairs)


def step(blocks, sections=0):
    return lambda s, b: (s + sections, b + blocks)


def back_two(s, b):
    x, z = divmod(b, 8)
    return s + 1, x * 8 + (z - 2) % 8


def back_four(s, b):
    x, u = divmod(b, 8)
    return s, x * 8 + (u + 2) % 8 + 4


def tile(q, k, v, bias):
    raw = lax.dot_general(q, k, (((1,), (1,)), ((), ())), preferred_element_type=jnp.float32)
    raw = raw + bias
    top = jnp.max(raw, axis=1, keepdims=True)
    weights = jnp.exp2((raw - top) * SCALE)
    total = jnp.sum(weights, axis=1, keepdims=True)
    out = jnp.dot(weights.astype(jnp.bfloat16), v, preferred_element_type=jnp.float32)
    return out, top, total


def merged(terms):
    highest = terms[0][1]
    for item in terms[1:]:
        highest = jnp.maximum(highest, item[1])
    out, total = None, None
    for tile_out, top, tile_sum in terms:
        factor = jnp.exp2((top - highest) * SCALE)
        part, part_sum = tile_out * factor, tile_sum * factor
        out = part if out is None else out + part
        total = part_sum if total is None else total + part_sum
    return out, highest, total


def bias_of(starts, first_key, height):
    keys = first_key + lax.broadcasted_iota(jnp.int32, (height, height), 1)
    return jnp.where(keys >= starts, 0.0, LOWEST)


def near_kernel(index_ref, starts_ref, q_ref, *refs):
    count = 3
    ks, vs = refs[:count], refs[count : 2 * count]
    acc_ref, stat_ref, bias_ref = refs[2 * count :]
    height = q_ref.shape[0]

    @pl.when(pl.program_id(0) == 0)
    def _():
        starts = starts_ref[:, :1]
        first = index_ref[0] * height
        rows = lax.broadcasted_iota(jnp.int32, (height, height), 0)
        columns = lax.broadcasted_iota(jnp.int32, (height, height), 1)
        bias_ref[0] = jnp.where(columns <= rows, bias_of(starts, first, height), LOWEST)
        for back in range(1, count):
            bias_ref[back] = bias_of(starts, first - back * height, height)

    for g in range(GROUP):
        q = q_ref[:, g * HDIM : (g + 1) * HDIM]
        terms = [tile(q, ks[i][...], vs[i][...], bias_ref[i]) for i in range(count)]
        out, top, total = merged(terms)
        acc_ref[:, g * HDIM : (g + 1) * HDIM] = out
        stat_ref[:, g : g + 1] = top
        stat_ref[:, 8 + g : 9 + g] = total


def far_kernel(index_ref, starts_ref, q_ref, *refs):
    count = 2
    ks, vs = refs[:count], refs[count : 2 * count]
    acc_ref, stat_ref, out_ref, bias_ref = refs[2 * count :]
    height = q_ref.shape[0]

    @pl.when(pl.program_id(0) == 0)
    def _():
        starts = starts_ref[:, :1]
        first = index_ref[0] * height
        for back in range(3, 3 + count):
            bias_ref[back - 3] = bias_of(starts, first - back * height, height)

    for g in range(GROUP):
        q = q_ref[:, g * HDIM : (g + 1) * HDIM]
        terms = [(acc_ref[:, g * HDIM : (g + 1) * HDIM], stat_ref[:, g : g + 1], stat_ref[:, 8 + g : 9 + g])]
        terms += [tile(q, ks[i][...], vs[i][...], bias_ref[i]) for i in range(count)]
        out, _, total = merged(terms)
        out_ref[:, g * HDIM : (g + 1) * HDIM] = (out * (1.0 / total)).astype(out_ref.dtype)


def specs(height, count):
    wide = pl.BlockSpec((height, GROUP * HDIM), lambda a: (0, a))
    narrow = pl.BlockSpec((height, HDIM), lambda a: (0, a))
    whole = pl.BlockSpec((height, HDIM), lambda a: (0, 0))
    return wide, narrow, [pl.BlockSpec(memory_space=pltpu.SMEM), whole, wide] + [narrow] * (2 * count)


def cost(height, count):
    pairs = KV_HEADS * GROUP * height * height * count
    return pl.CostEstimate(flops=4 * HDIM * pairs, transcendentals=pairs, bytes_accessed=8 << 20)


def near(index, starts, q, ks, vs):
    height = q.shape[0]
    wide, narrow, inputs = specs(height, 3)
    return pl.pallas_call(
        near_kernel,
        grid=(KV_HEADS,),
        in_specs=inputs,
        out_specs=[wide, narrow],
        out_shape=[
            jax.ShapeDtypeStruct(q.shape, jnp.float32),
            jax.ShapeDtypeStruct((height, KV_HEADS * HDIM), jnp.float32),
        ],
        scratch_shapes=[pltpu.VMEM((3, height, height), jnp.float32)],
        compiler_params=pltpu.CompilerParams(vmem_limit_bytes=40 << 20),
        cost_estimate=cost(height, 3),
        name="near_tiles",
    )(index, starts, q, *ks, *vs)


def far(index, starts, q, ks, vs, acc, stat):
    height = q.shape[0]
    wide, narrow, inputs = specs(height, 2)
    return pl.pallas_call(
        far_kernel,
        grid=(KV_HEADS,),
        in_specs=inputs + [wide, narrow],
        out_specs=wide,
        out_shape=jax.ShapeDtypeStruct(q.shape, jnp.bfloat16),
        scratch_shapes=[pltpu.VMEM((2, height, height), jnp.float32)],
        compiler_params=pltpu.CompilerParams(vmem_limit_bytes=40 << 20),
        cost_estimate=cost(height, 2),
        name="far_tiles",
    )(index, starts, q, *ks, *vs, acc, stat)


def first_starts(sizes, positions):
    order = jnp.arange(sizes.shape[0], dtype=jnp.int32)
    begins = jnp.sum(jnp.where(order[:, None] < order[None, :], sizes[:, None], 0), axis=0, dtype=jnp.int32)
    inside = begins[None, :] <= positions[:, None]
    return jnp.max(jnp.where(inside, begins[None, :], 0), axis=1)


def body(queries, keys, values, lengths):
    q, k, v = queries[0], keys[0], values[0]
    height = q.shape[0]
    index = lax.axis_index("seq").astype(jnp.int32)

    v_far = moved(v, back_two)
    k1 = moved(k, step(1, 1))
    v1 = moved(v, step(1, 1))
    q0 = moved(q, step(0, 1))
    k0 = moved(k, step(0, 1))
    v0 = moved(v, step(0, 1))
    sizes = moved(lengths, step(0, 1))[0]
    k2 = moved(k1, step(1))
    v2 = moved(v1, step(1))
    v4 = moved(v_far, back_four)
    k3 = moved(k2, step(1))
    v3 = moved(v4, step(-1))
    k4 = moved(k3, step(1))

    positions = index * height + jnp.arange(height, dtype=jnp.int32)
    starts = jnp.broadcast_to(first_starts(sizes, positions)[:, None], (height, HDIM))
    index = index.reshape(1)
    acc, stat = near(index, starts, q0, [k0, k1, k2], [v0, v1, v2])
    return far(index, starts, q0, [k3, k4], [v3, v4], acc, stat)[None]


def solution(mesh):
    return jax.shard_map(
        body,
        mesh=mesh,
        in_specs=(
            P("section", "seq", None),
            P("section", "seq", None),
            P("section", "seq", None),
            P("section", None),
        ),
        out_specs=P("section", "seq", None),
        check_vma=False,
    )
```

time: 147 us -> 84.3 us (0.57)
  the two profiles are of different devices: /device:TPU:68 before, /device:TPU:1 now
where the time goes in v1:
time: 84.3 us; the launch traced here: 84.2 us
  Pallas kernels  29.8 us (35%)
  starting transfers between devices  27.3 us (32%)
  waiting for transfers between devices  26.8 us (32%)
    ppermute x13, starting transfers between devices, moved(): return lax.ppermute(value, ('section', 'seq'), pairs)  27.3 us
    ppermute x13, waiting for transfers between devices, moved(): return lax.ppermute(value, ('section', 'seq'), pairs)  26.8 us
    pallas_call x1, Pallas kernels, far(): pl.pallas_call(far_kernel, grid=(KV_HEADS,), in_specs=inputs + [wide, nar...  20.5 us
    pallas_call x1, Pallas kernels, near(): pl.pallas_call(near_kernel, grid=(KV_HEADS,), in_specs=inputs, out_specs=...  9.29 us
  transfers between devices with their start and end apart: 13, of which 4 were waited for; matrix products, arithmetic and copies ran while one was open for 0% of the time, Pallas kernels for 11%

profile of v1, /device:TPU:1, one launch (start us, length us, event | category | flops | bytes accessed | tf_op | source)
XLA Modules:
  0.0 84.2 jit_solution(9807873434348692125)
XLA Ops:
  0.0 2.7 %collective-permute-start.1 = (bf16[256,2560]{1,0:T(8,128)(2,1)}, bf16[256,2560]{1,0:T(8,128)(2,1)S(1)}, u32[]{:S(2)}, u32[]{:S(2)}) collective-permute-start(bf16[256,2560]{1,0:T(8,128)(2,1)} %bitcast.6), channel_id=1, source_target_pairs={{0,32},{1,33},{2,34},{3,35},{4,36},{5,37},{6,38},{7,39},{8,40},{9,... | collective-permute-start | bytes 3932168 | tf_op jit(solution)/shard_map/ppermute | solution.py:25
  2.7 1.4 %collective-permute-start.2 = (bf16[256,512]{1,0:T(8,128)(2,1)}, bf16[256,512]{1,0:T(8,128)(2,1)S(1)}, u32[]{:S(2)}, u32[]{:S(2)}) collective-permute-start(bf16[256,512]{1,0:T(8,128)(2,1)} %bitcast.10), channel_id=1, source_target_pairs={{0,33},{1,34},{2,35},{3,36},{4,37},{5,38},{6,39},{7,40},{8,41},{9,... | collective-permute-start | bytes 786440 | tf_op jit(solution)/shard_map/ppermute | solution.py:25
  4.0 6.7 %collective-permute-start.6 = (bf16[256,512]{1,0:T(8,128)(2,1)}, bf16[256,512]{1,0:T(8,128)(2,1)S(1)}, u32[]{:S(2)}, u32[]{:S(2)}) collective-permute-start(bf16[256,512]{1,0:T(8,128)(2,1)} %bitcast.7), channel_id=1, source_target_pairs={{0,38},{1,39},{2,32},{3,33},{4,34},{5,35},{6,36},{7,37},{8,46},{9,... | collective-permute-start | bytes 786440 | tf_op jit(solution)/shard_map/ppermute | solution.py:25
  10.7 4.8 %collective-permute-done.2.refs_1_ = bf16[256,512]{1,0:T(8,128)(2,1)S(1)} collective-permute-done((bf16[256,512]{1,0:T(8,128)(2,1)}, bf16[256,512]{1,0:T(8,128)(2,1)S(1)}, u32[]{:S(2)}, u32[]{:S(2)}) %collective-permute-start.2) | collective-permute-done | bytes 262176 | tf_op jit(solution)/shard_map/ppermute | solution.py:25
  15.5 0.0 collective-permute-start.3
  15.5 2.5 %collective-permute-start = (s32[1,64]{1,0:T(1,128)}, s32[1,64]{1,0:T(1,128)S(1)}, u32[]{:S(2)}, u32[]{:S(2)}) collective-permute-start(s32[1,64]{1,0:T(1,128)} %param.7), channel_id=1, source_target_pairs={{0,32},{1,33},{2,34},{3,35},{4,36},{5,37},{6,38},{7,39},{8,40},{9,... | collective-permute-start | bytes 776 | tf_op jit(solution)/shard_map/ppermute | solution.py:25
  18.1 0.0 collective-permute-start.11
  18.1 5.1 %collective-permute-done = s32[1,64]{1,0:T(1,128)S(1)} collective-permute-done((s32[1,64]{1,0:T(1,128)}, s32[1,64]{1,0:T(1,128)S(1)}, u32[]{:S(2)}, u32[]{:S(2)}) %collective-permute-start) | collective-permute-done | bytes 288 | tf_op jit(solution)/shard_map/ppermute | solution.py:25
  23.2 2.4 %collective-permute-start.10 = (bf16[256,512]{1,0:T(8,128)(2,1)}, bf16[256,512]{1,0:T(8,128)(2,1)S(1)}, u32[]{:S(2)}, u32[]{:S(2)}) collective-permute-start(bf16[256,512]{1,0:T(8,128)(2,1)} %bitcast.9), channel_id=1, source_target_pairs={{0,32},{1,33},{2,34},{3,35},{4,36},{5,37},{6,38},{7,39},{8,40},{9,... | collective-permute-start | bytes 786440 | tf_op jit(solution)/shard_map/ppermute | solution.py:25
  25.6 0.0 collective-permute-done.6
  25.6 8.8 %collective-permute-start.7 = (bf16[256,512]{1,0:T(8,128)(2,1)S(1)}, bf16[256,512]{1,0:T(8,128)(2,1)S(1)}, u32[]{:S(2)}, u32[]{:S(2)}) collective-permute-start(bf16[256,512]{1,0:T(8,128)(2,1)S(1)} %collective-permute-done.6), channel_id=1, source_target_pairs={{0,6},{1,7},{2,8},{3,9},{4,10},{5,11},{6,4},{7,5},{8,14},{9,15},{1... | collective-permute-start | bytes 786440 | tf_op jit(solution)/shard_map/ppermute | solution.py:25
  34.4 0.0 collective-permute-done.3.refs_2_
  34.4 0.7 collective-permute-start.4
  35.2 0.0 collective-permute-done.11.refs_4_
  35.2 0.6 collective-permute-start.9
  35.8 0.0 collective-permute-done.10.refs_3_
  35.8 0.0 collective-permute-start.12
  35.8 0.1 select_reduce_fusion.1
  35.9 13.1 %collective-permute-done.7.refs_3_ = bf16[256,512]{1,0:T(8,128)(2,1)S(1)} collective-permute-done((bf16[256,512]{1,0:T(8,128)(2,1)S(1)}, bf16[256,512]{1,0:T(8,128)(2,1)S(1)}, u32[]{:S(2)}, u32[]{:S(2)}) %collective-permute-start.7) | collective-permute-done | bytes 262176 | tf_op jit(solution)/shard_map/ppermute | solution.py:25
  49.0 1.0 %collective-permute-start.8 = (bf16[256,512]{1,0:T(8,128)(2,1)S(1)}, bf16[256,512]{1,0:T(8,128)(2,1)S(1)}, u32[]{:S(2)}, u32[]{:S(2)}) collective-permute-start(bf16[256,512]{1,0:T(8,128)(2,1)S(1)} %collective-permute-done.7.refs_3_), channel_id=1, source_target_pairs={{0,31},{1,0},{2,1},{3,2},{4,3},{5,4},{6,5},{7,6},{8,7},{9,8},{10,9... | collective-permute-start | bytes 786440 | tf_op jit(solution)/shard_map/ppermute | solution.py:25
  50.0 0.0 collective-permute-done.4.refs_0_
  50.0 0.4 collective-permute-start.5
  50.4 0.1 select_reduce_fusion
  50.5 0.0 collective-permute-done.9.refs_0_
  50.5 3.7 %collective-permute-done.12.refs_5_ = bf16[256,512]{1,0:T(8,128)(2,1)S(1)} collective-permute-done((bf16[256,512]{1,0:T(8,128)(2,1)S(1)}, bf16[256,512]{1,0:T(8,128)(2,1)S(1)}, u32[]{:S(2)}, u32[]{:S(2)}) %collective-permute-start.12) | collective-permute-done | bytes 262176 | tf_op jit(solution)/shard_map/ppermute | solution.py:25
  54.3 0.0 collective-permute-done.1.q_ref
  54.3 0.1 broadcast_in_dim.42.starts_ref
  54.4 9.3 %near_tiles.1 = (f32[256,2560]{1,0:T(8,128)S(1)}, f32[256,512]{1,0:T(8,128)S(1)}) custom-call(s32[1]{0:T(128)} %bitcast.index_ref, s32[256,128]{1,0:T(8,128)S(1)} %broadcast_in_dim.42.starts_ref, bf16[256,2560]{1,0:T(8,128)(2,1)S(1)} %collective-permute-done.1.q_ref, bf16[256,512]{1,0:T(8,128)(2,1)S(1)} %collective-permute-done.9.refs_0_, ...), custom_call_target="tpu_custom_call" | custom-call | flops 2013265920 | bytes 8388608 | tf_op jit(solution)/shard_map/near_tiles/pallas_call | solution.py:131
  63.7 0.0 collective-permute-done.8.refs_2_
  63.7 0.0 collective-permute-done.5.refs_1_
  63.7 20.5 %far_tiles.1 = bf16[256,2560]{1,0:T(8,128)(2,1)} custom-call(s32[1]{0:T(128)} %bitcast.index_ref, s32[256,128]{1,0:T(8,128)S(1)} %broadcast_in_dim.42.starts_ref, bf16[256,2560]{1,0:T(8,128)(2,1)S(1)} %collective-permute-done.1.q_ref, bf16[256,512]{1,0:T(8,128)(2,1)S(1)} %collective-permute-done.4.refs_0_, ...), custom_call_target="tpu_custom_call" | custom-call | flops 1342177280 | bytes 8388608 | tf_op jit(solution)/shard_map/far_tiles/pallas_call | solution.py:150
  (1 shorter events, 0.0 us)
Async XLA Ops:
  0.0 54.3 %collective-permute-start.1 = (bf16[256,2560]{1,0:T(8,128)(2,1)}, bf16[256,2560]{1,0:T(8,128)(2,1)S(1)}, u32[]{:S(2)}, u32[]{:S(2)}) collective-permute-start(bf16[256,2560]{1,0:T(8,128)(2,1)} %bitcast.6), channel_id=1, source_target_pairs={{0,32},{1,33},{2,34},{3,35},{4,36},{5,37},{6,38},{7,39},{8,40},{9,... | collective-permute-start | bytes 3932168 | tf_op jit(solution)/shard_map/ppermute | solution.py:25
  2.7 12.8 %collective-permute-start.2 = (bf16[256,512]{1,0:T(8,128)(2,1)}, bf16[256,512]{1,0:T(8,128)(2,1)S(1)}, u32[]{:S(2)}, u32[]{:S(2)}) collective-permute-start(bf16[256,512]{1,0:T(8,128)(2,1)} %bitcast.10), channel_id=1, source_target_pairs={{0,33},{1,34},{2,35},{3,36},{4,37},{5,38},{6,39},{7,40},{8,41},{9,... | collective-permute-start | bytes 786440 | tf_op jit(solution)/shard_map/ppermute | solution.py:25
  4.0 21.6 %collective-permute-start.6 = (bf16[256,512]{1,0:T(8,128)(2,1)}, bf16[256,512]{1,0:T(8,128)(2,1)S(1)}, u32[]{:S(2)}, u32[]{:S(2)}) collective-permute-start(bf16[256,512]{1,0:T(8,128)(2,1)} %bitcast.7), channel_id=1, source_target_pairs={{0,38},{1,39},{2,32},{3,33},{4,34},{5,35},{6,36},{7,37},{8,46},{9,... | collective-permute-start | bytes 786440 | tf_op jit(solution)/shard_map/ppermute | solution.py:25
  15.5 18.9 %collective-permute-start.3 = (bf16[256,512]{1,0:T(8,128)(2,1)S(1)}, bf16[256,512]{1,0:T(8,128)(2,1)S(1)}, u32[]{:S(2)}, u32[]{:S(2)}) collective-permute-start(bf16[256,512]{1,0:T(8,128)(2,1)S(1)} %collective-permute-done.2.refs_1_), channel_id=1, source_target_pairs={{0,1},{1,2},{2,3},{3,4},{4,5},{5,6},{6,7},{7,8},{8,9},{9,10},{10,1... | collective-permute-start | bytes 786440 | tf_op jit(solution)/shard_map/ppermute | solution.py:25
  15.5 7.6 %collective-permute-start = (s32[1,64]{1,0:T(1,128)}, s32[1,64]{1,0:T(1,128)S(1)}, u32[]{:S(2)}, u32[]{:S(2)}) collective-permute-start(s32[1,64]{1,0:T(1,128)} %param.7), channel_id=1, source_target_pairs={{0,32},{1,33},{2,34},{3,35},{4,36},{5,37},{6,38},{7,39},{8,40},{9,... | collective-permute-start | bytes 776 | tf_op jit(solution)/shard_map/ppermute | solution.py:25
  18.1 17.1 %collective-permute-start.11 = (bf16[256,512]{1,0:T(8,128)(2,1)}, bf16[256,512]{1,0:T(8,128)(2,1)S(1)}, u32[]{:S(2)}, u32[]{:S(2)}) collective-permute-start(bf16[256,512]{1,0:T(8,128)(2,1)} %bitcast.8), channel_id=1, source_target_pairs={{0,33},{1,34},{2,35},{3,36},{4,37},{5,38},{6,39},{7,40},{8,41},{9,... | collective-permute-start | bytes 786440 | tf_op jit(solution)/shard_map/ppermute | solution.py:25
  23.2 12.6 %collective-permute-start.10 = (bf16[256,512]{1,0:T(8,128)(2,1)}, bf16[256,512]{1,0:T(8,128)(2,1)S(1)}, u32[]{:S(2)}, u32[]{:S(2)}) collective-permute-start(bf16[256,512]{1,0:T(8,128)(2,1)} %bitcast.9), channel_id=1, source_target_pairs={{0,32},{1,33},{2,34},{3,35},{4,36},{5,37},{6,38},{7,39},{8,40},{9,... | collective-permute-start | bytes 786440 | tf_op jit(solution)/shard_map/ppermute | solution.py:25
  25.6 23.4 %collective-permute-start.7 = (bf16[256,512]{1,0:T(8,128)(2,1)S(1)}, bf16[256,512]{1,0:T(8,128)(2,1)S(1)}, u32[]{:S(2)}, u32[]{:S(2)}) collective-permute-start(bf16[256,512]{1,0:T(8,128)(2,1)S(1)} %collective-permute-done.6), channel_id=1, source_target_pairs={{0,6},{1,7},{2,8},{3,9},{4,10},{5,11},{6,4},{7,5},{8,14},{9,15},{1... | collective-permute-start | bytes 786440 | tf_op jit(solution)/shard_map/ppermute | solution.py:25
  34.4 15.6 %collective-permute-start.4 = (bf16[256,512]{1,0:T(8,128)(2,1)S(1)}, bf16[256,512]{1,0:T(8,128)(2,1)S(1)}, u32[]{:S(2)}, u32[]{:S(2)}) collective-permute-start(bf16[256,512]{1,0:T(8,128)(2,1)S(1)} %collective-permute-done.3.refs_2_), channel_id=1, source_target_pairs={{0,1},{1,2},{2,3},{3,4},{4,5},{5,6},{6,7},{7,8},{8,9},{9,10},{10,1... | collective-permute-start | bytes 786440 | tf_op jit(solution)/shard_map/ppermute | solution.py:25
  35.2 15.3 %collective-permute-start.9 = (bf16[256,512]{1,0:T(8,128)(2,1)}, bf16[256,512]{1,0:T(8,128)(2,1)S(1)}, u32[]{:S(2)}, u32[]{:S(2)}) collective-permute-start(bf16[256,512]{1,0:T(8,128)(2,1)} %bitcast.11), channel_id=1, source_target_pairs={{0,32},{1,33},{2,34},{3,35},{4,36},{5,37},{6,38},{7,39},{8,40},{9,... | collective-permute-start | bytes 786440 | tf_op jit(solution)/shard_map/ppermute | solution.py:25
  35.8 18.5 %collective-permute-start.12 = (bf16[256,512]{1,0:T(8,128)(2,1)S(1)}, bf16[256,512]{1,0:T(8,128)(2,1)S(1)}, u32[]{:S(2)}, u32[]{:S(2)}) collective-permute-start(bf16[256,512]{1,0:T(8,128)(2,1)S(1)} %collective-permute-done.11.refs_4_), channel_id=1, source_target_pairs={{0,1},{1,2},{2,3},{3,4},{4,5},{5,6},{6,7},{7,8},{8,9},{9,10},{10,1... | collective-permute-start | bytes 786440 | tf_op jit(solution)/shard_map/ppermute | solution.py:25
  49.0 14.7 %collective-permute-start.8 = (bf16[256,512]{1,0:T(8,128)(2,1)S(1)}, bf16[256,512]{1,0:T(8,128)(2,1)S(1)}, u32[]{:S(2)}, u32[]{:S(2)}) collective-permute-start(bf16[256,512]{1,0:T(8,128)(2,1)S(1)} %collective-permute-done.7.refs_3_), channel_id=1, source_target_pairs={{0,31},{1,0},{2,1},{3,2},{4,3},{5,4},{6,5},{7,6},{8,7},{9,8},{10,9... | collective-permute-start | bytes 786440 | tf_op jit(solution)/shard_map/ppermute | solution.py:25
  50.0 13.7 %collective-permute-start.5 = (bf16[256,512]{1,0:T(8,128)(2,1)S(1)}, bf16[256,512]{1,0:T(8,128)(2,1)S(1)}, u32[]{:S(2)}, u32[]{:S(2)}) collective-permute-start(bf16[256,512]{1,0:T(8,128)(2,1)S(1)} %collective-permute-done.4.refs_0_), channel_id=1, source_target_pairs={{0,1},{1,2},{2,3},{3,4},{4,5},{5,6},{6,7},{7,8},{8,9},{9,10},{10,1... | collective-permute-start | bytes 786440 | tf_op jit(solution)/shard_map/ppermute | solution.py:25

commit v2 on v1

v2 whole, which is shorter than its diff:
```python
from functools import partial

import jax
import jax.numpy as jnp
from jax import lax
from jax.experimental import pallas as pl
from jax.experimental.pallas import tpu as pltpu
from jax.sharding import PartitionSpec as P

HDIM = 128
KV_HEADS = 4
GROUP = 5
REACH = 4
LOWEST = -1e30
SCALE = HDIM**-0.5 * 1.4426950408889634


def moved(value, route):
    sections, blocks = lax.axis_size("section"), lax.axis_size("seq")
    pairs = []
    for s in range(sections):
        for b in range(blocks):
            s2, b2 = route(s, b)
            pairs.append((s * blocks + b, (s2 % sections) * blocks + b2 % blocks))
    return lax.ppermute(value, ("section", "seq"), pairs)


def step(blocks, sections=0):
    return lambda s, b: (s + sections, b + blocks)


def back_two(s, b):
    x, z = divmod(b, 8)
    return s + 1, x * 8 + (z - 2) % 8


def back_four(s, b):
    x, u = divmod(b, 8)
    return s, x * 8 + (u + 2) % 8 + 4


def bias_of(starts, first_key, height):
    keys = first_key + lax.broadcasted_iota(jnp.int32, (height, height), 1)
    return jnp.where(keys >= starts, 0.0, LOWEST)


def tile(q, k, v, bias):
    height = bias.shape[0]
    raw = lax.dot_general(q, k, (((1,), (1,)), ((), ())), preferred_element_type=jnp.float32)
    raw = (raw.reshape(GROUP, height, height) + bias[None]).reshape(GROUP * height, height)
    top = jnp.max(raw, axis=1, keepdims=True)
    weights = jnp.exp2((raw - top) * SCALE)
    total = jnp.sum(weights, axis=1, keepdims=True)
    out = jnp.dot(weights.astype(jnp.bfloat16), v, preferred_element_type=jnp.float32)
    wide = (GROUP * height, HDIM)
    return out, jnp.broadcast_to(top, wide), jnp.broadcast_to(total, wide)


def merged(terms):
    highest = terms[0][1]
    for item in terms[1:]:
        highest = jnp.maximum(highest, item[1])
    out, total = None, None
    for tile_out, top, tile_sum in terms:
        factor = jnp.exp2((top - highest) * SCALE)
        part, part_sum = tile_out * factor, tile_sum * factor
        out = part if out is None else out + part
        total = part_sum if total is None else total + part_sum
    return out, highest, total


def kernel(backs, opening, closing, index_ref, starts_ref, q_ref, *refs):
    count = len(backs)
    ks, vs, refs = refs[:count], refs[count : 2 * count], refs[2 * count :]
    state_in = () if opening else refs[:3]
    outs, bias_ref = refs[len(state_in) : -1], refs[-1]
    height = q_ref.shape[0]
    starts = starts_ref[:, :1]
    first = index_ref[0] * height
    for i, back in enumerate(backs):
        bias = bias_of(starts, first - back * height, height)
        if back == 0:
            rows = lax.broadcasted_iota(jnp.int32, (height, height), 0)
            columns = lax.broadcasted_iota(jnp.int32, (height, height), 1)
            bias = jnp.where(columns <= rows, bias, LOWEST)
        bias_ref[i] = bias

    @pl.loop(0, KV_HEADS)
    def _(a):
        lanes = pl.ds(pl.multiple_of(a * HDIM, HDIM), HDIM)
        heads = [
            pl.ds(pl.multiple_of((a * GROUP + g) * HDIM, HDIM), HDIM) for g in range(GROUP)
        ]
        q = jnp.concatenate([q_ref[:, h] for h in heads], axis=0)
        terms = [tuple(ref[a] for ref in state_in)] if state_in else []
        terms += [tile(q, ks[i][:, lanes], vs[i][:, lanes], bias_ref[i]) for i in range(count)]
        result = merged(terms)
        if closing:
            done = (result[0] / result[2]).astype(jnp.bfloat16)
            for g in range(GROUP):
                outs[0][:, heads[g]] = done[g * height : (g + 1) * height]
        else:
            for ref, part in zip(outs, result):
                ref[a] = part


def attention(backs, index, starts, q, ks, vs, state=(), closing=False):
    height = q.shape[0]
    count = len(backs)
    pairs = KV_HEADS * GROUP * height * height * count
    vmem = pl.BlockSpec(memory_space=pltpu.VMEM)
    part = jax.ShapeDtypeStruct((KV_HEADS, GROUP * height, HDIM), jnp.float32)
    return pl.pallas_call(
        partial(kernel, backs, not state, closing),
        in_specs=[pl.BlockSpec(memory_space=pltpu.SMEM)] + [vmem] * (2 + 2 * count + len(state)),
        out_specs=vmem if closing else [vmem] * 3,
        out_shape=jax.ShapeDtypeStruct(q.shape, jnp.bfloat16) if closing else [part] * 3,
        scratch_shapes=[pltpu.VMEM((count, height, height), jnp.float32)],
        compiler_params=pltpu.CompilerParams(vmem_limit_bytes=12 << 20),
        cost_estimate=pl.CostEstimate(
            flops=4 * HDIM * pairs, transcendentals=pairs, bytes_accessed=8 << 20
        ),
        name="tiles_" + "_".join(str(back) for back in backs),
    )(index, starts, q, *ks, *vs, *state)


def first_starts(sizes, positions):
    order = jnp.arange(sizes.shape[0], dtype=jnp.int32)
    begins = jnp.sum(jnp.where(order[:, None] < order[None, :], sizes[:, None], 0), axis=0, dtype=jnp.int32)
    inside = begins[None, :] <= positions[:, None]
    return jnp.max(jnp.where(inside, begins[None, :], 0), axis=1)


def body(queries, keys, values, lengths):
    q, k, v = queries[0], keys[0], values[0]
    height = q.shape[0]
    index = lax.axis_index("seq").astype(jnp.int32)

    sizes = moved(lengths, step(0, 1))
    v_far = moved(v, back_two)
    k1 = moved(k, step(1, 1))
    v1 = moved(v, step(1, 1))
    q, k, v, sizes = lax.optimization_barrier((q, k, v, sizes))
    q0 = moved(q, step(0, 1))
    k0 = moved(k, step(0, 1))
    v0 = moved(v, step(0, 1))
    k2 = moved(k1, step(1))
    v2 = moved(v1, step(1))
    v4 = moved(v_far, back_four)
    k3 = moved(k2, step(1))
    v3 = moved(v4, step(-1))
    k4 = moved(k3, step(1))

    positions = index * height + jnp.arange(height, dtype=jnp.int32)
    starts = jnp.broadcast_to(first_starts(sizes[0], positions)[:, None], (height, HDIM))
    index = index.reshape(1)
    state = attention((0, 1, 2), index, starts, q0, [k0, k1, k2], [v0, v1, v2])
    return attention((3, 4), index, starts, q0, [k3, k4], [v3, v4], state, True)[None]


def solution(mesh):
    return jax.shard_map(
        body,
        mesh=mesh,
        in_specs=(
            P("section", "seq", None),
            P("section", "seq", None),
            P("section", "seq", None),
            P("section", None),
        ),
        out_specs=P("section", "seq", None),
        check_vma=False,
    )
```

time: 84.3 us -> 71.6 us (0.85)
  Pallas kernels: 29.8 us -> 14.9 us
  waiting for transfers between devices: 26.8 us -> 33.6 us
  starting transfers between devices: 27.3 us -> 22.7 us
    pallas_call x2, Pallas kernels: 29.8 us -> 14.9 us  [attention(): pl.pallas_call(partial(kernel, backs, not state, closing), in_specs=[pl.B...]
    ppermute x13, waiting for transfers between devices: 26.8 us -> 33.6 us  [moved(): return lax.ppermute(value, ('section', 'seq'), pairs)]
    ppermute x13, starting transfers between devices: 27.3 us -> 22.7 us  [moved(): return lax.ppermute(value, ('section', 'seq'), pairs)]
  transfers between devices with their start and end apart: 13 -> 13, of which waited for: 4 -> 6; matrix products, arithmetic and copies ran while one was open for 0% -> 0% of each run, Pallas kernels for 11% -> 10%
where the time goes in v2:
time: 71.6 us; the launch traced here: 71.5 us
  waiting for transfers between devices  33.6 us (47%)
  starting transfers between devices  22.7 us (32%)
  Pallas kernels  14.9 us (21%)
    ppermute x13, waiting for transfers between devices, moved(): return lax.ppermute(value, ('section', 'seq'), pairs)  33.6 us
    ppermute x13, starting transfers between devices, moved(): return lax.ppermute(value, ('section', 'seq'), pairs)  22.7 us
    pallas_call x2, Pallas kernels, attention(): pl.pallas_call(partial(kernel, backs, not state, closing), in_specs=[pl.B...  14.9 us
  transfers between devices with their start and end apart: 13, of which 6 were waited for; matrix products, arithmetic and copies ran while one was open for 0% of the time, Pallas kernels for 10%

profile of v2, /device:TPU:1, one launch (start us, length us, event | category | flops | bytes accessed | tf_op | source)
XLA Modules:
  0.0 71.5 jit_solution(17133278489172471029)
XLA Ops:
  0.0 2.7 %collective-permute-start = (s32[1,64]{1,0:T(1,128)}, s32[1,64]{1,0:T(1,128)S(1)}, u32[]{:S(2)}, u32[]{:S(2)}) collective-permute-start(s32[1,64]{1,0:T(1,128)} %param.7), channel_id=1, source_target_pairs={{0,32},{1,33},{2,34},{3,35},{4,36},{5,37},{6,38},{7,39},{8,40},{9,... | collective-permute-start | bytes 776 | tf_op jit(solution)/shard_map/ppermute | solution.py:25
  2.7 1.3 %collective-permute-done = s32[1,64]{1,0:T(1,128)S(1)} collective-permute-done((s32[1,64]{1,0:T(1,128)}, s32[1,64]{1,0:T(1,128)S(1)}, u32[]{:S(2)}, u32[]{:S(2)}) %collective-permute-start) | collective-permute-done | bytes 288 | tf_op jit(solution)/shard_map/ppermute | solution.py:25
  4.0 1.8 %collective-permute-start.1 = (bf16[256,2560]{1,0:T(8,128)(2,1)}, bf16[256,2560]{1,0:T(8,128)(2,1)S(1)}, u32[]{:S(2)}, u32[]{:S(2)}) collective-permute-start(bf16[256,2560]{1,0:T(8,128)(2,1)} %bitcast.6), channel_id=1, source_target_pairs={{0,32},{1,33},{2,34},{3,35},{4,36},{5,37},{6,38},{7,39},{8,40},{9,... | collective-permute-start | bytes 3932168 | tf_op jit(solution)/shard_map/ppermute | solution.py:25
  5.8 1.4 %collective-permute-start.2 = (bf16[256,512]{1,0:T(8,128)(2,1)}, bf16[256,512]{1,0:T(8,128)(2,1)S(1)}, u32[]{:S(2)}, u32[]{:S(2)}) collective-permute-start(bf16[256,512]{1,0:T(8,128)(2,1)} %bitcast.10), channel_id=1, source_target_pairs={{0,33},{1,34},{2,35},{3,36},{4,37},{5,38},{6,39},{7,40},{8,41},{9,... | collective-permute-start | bytes 786440 | tf_op jit(solution)/shard_map/ppermute | solution.py:25
  7.1 6.7 %collective-permute-start.6 = (bf16[256,512]{1,0:T(8,128)(2,1)}, bf16[256,512]{1,0:T(8,128)(2,1)S(1)}, u32[]{:S(2)}, u32[]{:S(2)}) collective-permute-start(bf16[256,512]{1,0:T(8,128)(2,1)} %bitcast.7), channel_id=1, source_target_pairs={{0,38},{1,39},{2,32},{3,33},{4,34},{5,35},{6,36},{7,37},{8,46},{9,... | collective-permute-start | bytes 786440 | tf_op jit(solution)/shard_map/ppermute | solution.py:25
  13.8 6.8 %collective-permute-done.2.refs_1_ = bf16[256,512]{1,0:T(8,128)(2,1)S(1)} collective-permute-done((bf16[256,512]{1,0:T(8,128)(2,1)}, bf16[256,512]{1,0:T(8,128)(2,1)S(1)}, u32[]{:S(2)}, u32[]{:S(2)}) %collective-permute-start.2) | collective-permute-done | bytes 262176 | tf_op jit(solution)/shard_map/ppermute | solution.py:25
  20.6 0.0 collective-permute-start.3
  20.6 0.0 collective-permute-start.11
  20.6 1.3 %collective-permute-start.10 = (bf16[256,512]{1,0:T(8,128)(2,1)}, bf16[256,512]{1,0:T(8,128)(2,1)S(1)}, u32[]{:S(2)}, u32[]{:S(2)}) collective-permute-start(bf16[256,512]{1,0:T(8,128)(2,1)} %bitcast.9), channel_id=1, source_target_pairs={{0,32},{1,33},{2,34},{3,35},{4,36},{5,37},{6,38},{7,39},{8,40},{9,... | collective-permute-start | bytes 786440 | tf_op jit(solution)/shard_map/ppermute | solution.py:25
  21.9 2.8 %collective-permute-done.6 = bf16[256,512]{1,0:T(8,128)(2,1)S(1)} collective-permute-done((bf16[256,512]{1,0:T(8,128)(2,1)}, bf16[256,512]{1,0:T(8,128)(2,1)S(1)}, u32[]{:S(2)}, u32[]{:S(2)}) %collective-permute-start.6) | collective-permute-done | bytes 262176 | tf_op jit(solution)/shard_map/ppermute | solution.py:25
  24.6 4.1 %collective-permute-start.7 = (bf16[256,512]{1,0:T(8,128)(2,1)S(1)}, bf16[256,512]{1,0:T(8,128)(2,1)S(1)}, u32[]{:S(2)}, u32[]{:S(2)}) collective-permute-start(bf16[256,512]{1,0:T(8,128)(2,1)S(1)} %collective-permute-done.6), channel_id=1, source_target_pairs={{0,6},{1,7},{2,8},{3,9},{4,10},{5,11},{6,4},{7,5},{8,14},{9,15},{1... | collective-permute-start | bytes 786440 | tf_op jit(solution)/shard_map/ppermute | solution.py:25
  28.7 0.9 %collective-permute-done.3.refs_2_ = bf16[256,512]{1,0:T(8,128)(2,1)S(1)} collective-permute-done((bf16[256,512]{1,0:T(8,128)(2,1)S(1)}, bf16[256,512]{1,0:T(8,128)(2,1)S(1)}, u32[]{:S(2)}, u32[]{:S(2)}) %collective-permute-start.3) | collective-permute-done | bytes 262176 | tf_op jit(solution)/shard_map/ppermute | solution.py:25
  29.7 0.0 collective-permute-start.4
  29.7 16.2 %collective-permute-done.11.refs_4_ = bf16[256,512]{1,0:T(8,128)(2,1)S(1)} collective-permute-done((bf16[256,512]{1,0:T(8,128)(2,1)}, bf16[256,512]{1,0:T(8,128)(2,1)S(1)}, u32[]{:S(2)}, u32[]{:S(2)}) %collective-permute-start.11) | collective-permute-done | bytes 262176 | tf_op jit(solution)/shard_map/ppermute | solution.py:25
  45.8 0.0 collective-permute-start.9
  45.8 0.0 collective-permute-done.10.refs_3_
  45.8 0.0 collective-permute-start.12
  45.9 0.1 select_reduce_fusion.1
  45.9 0.0 collective-permute-done.7.refs_3_
  46.0 4.8 %collective-permute-start.8 = (bf16[256,512]{1,0:T(8,128)(2,1)S(1)}, bf16[256,512]{1,0:T(8,128)(2,1)S(1)}, u32[]{:S(2)}, u32[]{:S(2)}) collective-permute-start(bf16[256,512]{1,0:T(8,128)(2,1)S(1)} %collective-permute-done.7.refs_3_), channel_id=1, source_target_pairs={{0,31},{1,0},{2,1},{3,2},{4,3},{5,4},{6,5},{7,6},{8,7},{9,8},{10,9... | collective-permute-start | bytes 786440 | tf_op jit(solution)/shard_map/ppermute | solution.py:25
  50.8 0.0 collective-permute-done.4.refs_0_
  50.8 0.0 collective-permute-start.5
  50.8 0.1 select_reduce_fusion
  50.9 0.0 collective-permute-done.9.refs_0_
  50.9 5.6 %collective-permute-done.12.refs_5_ = bf16[256,512]{1,0:T(8,128)(2,1)S(1)} collective-permute-done((bf16[256,512]{1,0:T(8,128)(2,1)S(1)}, bf16[256,512]{1,0:T(8,128)(2,1)S(1)}, u32[]{:S(2)}, u32[]{:S(2)}) %collective-permute-start.12) | collective-permute-done | bytes 262176 | tf_op jit(solution)/shard_map/ppermute | solution.py:25
  56.5 0.0 collective-permute-done.1.q_ref
  56.5 0.1 broadcast_in_dim.42.starts_ref
  56.6 7.2 %tiles_0_1_2.1 = (f32[4,1280,128]{2,1,0:T(8,128)S(1)}, f32[4,1280,128]{2,1,0:T(8,128)S(1)}, f32[4,1280,128]{2,1,0:T(8,128)S(1)}) custom-call(s32[1]{0:T(128)} %bitcast.index_ref, s32[256,128]{1,0:T(8,128)S(1)} %broadcast_in_dim.42.starts_ref, bf16[256,2560]{1,0:T(8,128)(2,1)S(1)} %collective-permute-done.1.q_ref, ...), custom_call_target="tpu_custom_call" | custom-call | flops 2013265920 | bytes 8388608 | tf_op jit(solution)/shard_map/tiles_0_1_2/pallas_call | solution.py:113
  63.9 0.0 collective-permute-done.8.refs_2_
  63.9 0.0 collective-permute-done.5.refs_1_
  63.9 7.6 %tiles_3_4.1 = bf16[256,2560]{1,0:T(8,128)(2,1)} custom-call(s32[1]{0:T(128)} %bitcast.index_ref, s32[256,128]{1,0:T(8,128)S(1)} %broadcast_in_dim.42.starts_ref, bf16[256,2560]{1,0:T(8,128)(2,1)S(1)} %collective-permute-done.1.q_ref, bf16[256,512]{1,0:T(8,128)(2,1)S(1)} %collective-permute-done.4.refs_0_, ...), custom_call_target="tpu_custom_call" | custom-call | flops 1342177280 | bytes 8388608 | tf_op jit(solution)/shard_map/tiles_3_4/pallas_call | solution.py:113
  (1 shorter events, 0.0 us)
Async XLA Ops:
  0.0 4.0 %collective-permute-start = (s32[1,64]{1,0:T(1,128)}, s32[1,64]{1,0:T(1,128)S(1)}, u32[]{:S(2)}, u32[]{:S(2)}) collective-permute-start(s32[1,64]{1,0:T(1,128)} %param.7), channel_id=1, source_target_pairs={{0,32},{1,33},{2,34},{3,35},{4,36},{5,37},{6,38},{7,39},{8,40},{9,... | collective-permute-start | bytes 776 | tf_op jit(solution)/shard_map/ppermute | solution.py:25
  4.0 52.5 %collective-permute-start.1 = (bf16[256,2560]{1,0:T(8,128)(2,1)}, bf16[256,2560]{1,0:T(8,128)(2,1)S(1)}, u32[]{:S(2)}, u32[]{:S(2)}) collective-permute-start(bf16[256,2560]{1,0:T(8,128)(2,1)} %bitcast.6), channel_id=1, source_target_pairs={{0,32},{1,33},{2,34},{3,35},{4,36},{5,37},{6,38},{7,39},{8,40},{9,... | collective-permute-start | bytes 3932168 | tf_op jit(solution)/shard_map/ppermute | solution.py:25
  5.8 14.8 %collective-permute-start.2 = (bf16[256,512]{1,0:T(8,128)(2,1)}, bf16[256,512]{1,0:T(8,128)(2,1)S(1)}, u32[]{:S(2)}, u32[]{:S(2)}) collective-permute-start(bf16[256,512]{1,0:T(8,128)(2,1)} %bitcast.10), channel_id=1, source_target_pairs={{0,33},{1,34},{2,35},{3,36},{4,37},{5,38},{6,39},{7,40},{8,41},{9,... | collective-permute-start | bytes 786440 | tf_op jit(solution)/shard_map/ppermute | solution.py:25
  7.1 17.5 %collective-permute-start.6 = (bf16[256,512]{1,0:T(8,128)(2,1)}, bf16[256,512]{1,0:T(8,128)(2,1)S(1)}, u32[]{:S(2)}, u32[]{:S(2)}) collective-permute-start(bf16[256,512]{1,0:T(8,128)(2,1)} %bitcast.7), channel_id=1, source_target_pairs={{0,38},{1,39},{2,32},{3,33},{4,34},{5,35},{6,36},{7,37},{8,46},{9,... | collective-permute-start | bytes 786440 | tf_op jit(solution)/shard_map/ppermute | solution.py:25
  20.6 9.0 %collective-permute-start.3 = (bf16[256,512]{1,0:T(8,128)(2,1)S(1)}, bf16[256,512]{1,0:T(8,128)(2,1)S(1)}, u32[]{:S(2)}, u32[]{:S(2)}) collective-permute-start(bf16[256,512]{1,0:T(8,128)(2,1)S(1)} %collective-permute-done.2.refs_1_), channel_id=1, source_target_pairs={{0,1},{1,2},{2,3},{3,4},{4,5},{5,6},{6,7},{7,8},{8,9},{9,10},{10,1... | collective-permute-start | bytes 786440 | tf_op jit(solution)/shard_map/ppermute | solution.py:25
  20.6 25.2 %collective-permute-start.11 = (bf16[256,512]{1,0:T(8,128)(2,1)}, bf16[256,512]{1,0:T(8,128)(2,1)S(1)}, u32[]{:S(2)}, u32[]{:S(2)}) collective-permute-start(bf16[256,512]{1,0:T(8,128)(2,1)} %bitcast.8), channel_id=1, source_target_pairs={{0,33},{1,34},{2,35},{3,36},{4,37},{5,38},{6,39},{7,40},{8,41},{9,... | collective-permute-start | bytes 786440 | tf_op jit(solution)/shard_map/ppermute | solution.py:25
  20.6 25.2 %collective-permute-start.10 = (bf16[256,512]{1,0:T(8,128)(2,1)}, bf16[256,512]{1,0:T(8,128)(2,1)S(1)}, u32[]{:S(2)}, u32[]{:S(2)}) collective-permute-start(bf16[256,512]{1,0:T(8,128)(2,1)} %bitcast.9), channel_id=1, source_target_pairs={{0,32},{1,33},{2,34},{3,35},{4,36},{5,37},{6,38},{7,39},{8,40},{9,... | collective-permute-start | bytes 786440 | tf_op jit(solution)/shard_map/ppermute | solution.py:25
  24.6 21.3 %collective-permute-start.7 = (bf16[256,512]{1,0:T(8,128)(2,1)S(1)}, bf16[256,512]{1,0:T(8,128)(2,1)S(1)}, u32[]{:S(2)}, u32[]{:S(2)}) collective-permute-start(bf16[256,512]{1,0:T(8,128)(2,1)S(1)} %collective-permute-done.6), channel_id=1, source_target_pairs={{0,6},{1,7},{2,8},{3,9},{4,10},{5,11},{6,4},{7,5},{8,14},{9,15},{1... | collective-permute-start | bytes 786440 | tf_op jit(solution)/shard_map/ppermute | solution.py:25
  29.7 21.1 %collective-permute-start.4 = (bf16[256,512]{1,0:T(8,128)(2,1)S(1)}, bf16[256,512]{1,0:T(8,128)(2,1)S(1)}, u32[]{:S(2)}, u32[]{:S(2)}) collective-permute-start(bf16[256,512]{1,0:T(8,128)(2,1)S(1)} %collective-permute-done.3.refs_2_), channel_id=1, source_target_pairs={{0,1},{1,2},{2,3},{3,4},{4,5},{5,6},{6,7},{7,8},{8,9},{9,10},{10,1... | collective-permute-start | bytes 786440 | tf_op jit(solution)/shard_map/ppermute | solution.py:25
  45.8 5.1 %collective-permute-start.9 = (bf16[256,512]{1,0:T(8,128)(2,1)}, bf16[256,512]{1,0:T(8,128)(2,1)S(1)}, u32[]{:S(2)}, u32[]{:S(2)}) collective-permute-start(bf16[256,512]{1,0:T(8,128)(2,1)} %bitcast.11), channel_id=1, source_target_pairs={{0,32},{1,33},{2,34},{3,35},{4,36},{5,37},{6,38},{7,39},{8,40},{9,... | collective-permute-start | bytes 786440 | tf_op jit(solution)/shard_map/ppermute | solution.py:25
  45.8 10.7 %collective-permute-start.12 = (bf16[256,512]{1,0:T(8,128)(2,1)S(1)}, bf16[256,512]{1,0:T(8,128)(2,1)S(1)}, u32[]{:S(2)}, u32[]{:S(2)}) collective-permute-start(bf16[256,512]{1,0:T(8,128)(2,1)S(1)} %collective-permute-done.11.refs_4_), channel_id=1, source_target_pairs={{0,1},{1,2},{2,3},{3,4},{4,5},{5,6},{6,7},{7,8},{8,9},{9,10},{10,1... | collective-permute-start | bytes 786440 | tf_op jit(solution)/shard_map/ppermute | solution.py:25
  46.0 17.9 %collective-permute-start.8 = (bf16[256,512]{1,0:T(8,128)(2,1)S(1)}, bf16[256,512]{1,0:T(8,128)(2,1)S(1)}, u32[]{:S(2)}, u32[]{:S(2)}) collective-permute-start(bf16[256,512]{1,0:T(8,128)(2,1)S(1)} %collective-permute-done.7.refs_3_), channel_id=1, source_target_pairs={{0,31},{1,0},{2,1},{3,2},{4,3},{5,4},{6,5},{7,6},{8,7},{9,8},{10,9... | collective-permute-start | bytes 786440 | tf_op jit(solution)/shard_map/ppermute | solution.py:25
  50.8 13.1 %collective-permute-start.5 = (bf16[256,512]{1,0:T(8,128)(2,1)S(1)}, bf16[256,512]{1,0:T(8,128)(2,1)S(1)}, u32[]{:S(2)}, u32[]{:S(2)}) collective-permute-start(bf16[256,512]{1,0:T(8,128)(2,1)S(1)} %collective-permute-done.4.refs_0_), channel_id=1, source_target_pairs={{0,1},{1,2},{2,3},{3,4},{4,5},{5,6},{6,7},{7,8},{8,9},{9,10},{10,1... | collective-permute-start | bytes 786440 | tf_op jit(solution)/shard_map/ppermute | solution.py:25
